TPU v7x, 32 devices: a whole 2x2x4 slice. The times are simulated.
32 devices in a mesh: row: 4 (over z), col: 8 (over y, x, core).
Axes of the slice: x: 2, y: 2, z: 4, core: 2. Of those that a mesh axis runs over, the one named last changes fastest.
Arguments:
- amplitudes: bfloat16 [16384, 16384], P('row', 'col'), may hold values from -0.046875 to 0.046875
- accumulated: float32 [16384, 16384], P('row', 'col'), may hold values from -6 to 6
- cholesky: bfloat16 [16384, 1536], P(('row', 'col')), may hold values from -1.5 to 1.5
- occ_index: int32 [16384], replicated, may hold values from 0 to 63
- vir_index: int32 [16384], replicated, may hold values from 0 to 255
- occ_energy: float32 [64], replicated, may hold values from -3 to -0.5
- vir_energy: float32 [256], replicated, may hold values from 0.5 to 4
Outputs:
- updated: float32 [16384, 16384], P('row', 'col')
All inputs are finite; a program needn't handle non-finite values.
Results may differ from a plain program's by a relative error of at most 0.0022.
Values may be sent and summed in bfloat16 or wider, within the bound.
A program may use at most 192 MiB of HBM per device.

v0:
```python
import jax
import jax.numpy as jnp
from jax import lax
from jax.sharding import PartitionSpec as P


def spread(value, axis, source):
    kept = jnp.where(lax.axis_index(axis) == source, value, 0).astype(value.dtype)
    return lax.psum(kept, axis)


def lookup(index, table):
    hits = index[:, None] == jnp.arange(table.shape[0], dtype=jnp.int32)[None, :]
    return jnp.sum(jnp.where(hits, table[None, :], jnp.zeros((), table.dtype)), axis=1)


def on_device(amplitudes, accumulated, cholesky, occ_index, vir_index, occ_energy, vir_energy):
    row_count = lax.axis_size("row")
    col_count = lax.axis_size("col")
    ratio = col_count // row_count
    row_rank = lax.axis_index("row")
    col_rank = lax.axis_index("col")
    row_block = amplitudes.shape[0]
    col_block = amplitudes.shape[1]
    owner = col_rank // ratio
    offset = col_rank % ratio * col_block
    b_rows = lax.all_gather(cholesky, "col", axis=0, tiled=True)
    b_half = lax.dynamic_slice_in_dim(b_rows, offset, col_block, 0)
    b_cols = spread(b_half, "row", owner)
    summed = lax.psum_scatter(
        jnp.dot(amplitudes, b_cols, preferred_element_type=jnp.float32),
        "col",
        scatter_dimension=0,
        tiled=True,
    )
    x_piece = (cholesky.astype(jnp.float32) + summed).astype(jnp.bfloat16)
    x_rows = lax.all_gather(x_piece, "col", axis=0, tiled=True)
    x_half = lax.dynamic_slice_in_dim(x_rows, offset, col_block, 0)
    x_cols = spread(x_half, "row", owner)
    product = lax.dot_general(
        x_rows, x_cols, (((1,), (1,)), ((), ())), preferred_element_type=jnp.float32
    )
    occ_rows = lax.dynamic_slice_in_dim(occ_index, row_rank * row_block, row_block, 0)
    vir_rows = lax.dynamic_slice_in_dim(vir_index, row_rank * row_block, row_block, 0)
    occ_cols = lax.dynamic_slice_in_dim(occ_index, col_rank * col_block, col_block, 0)
    vir_cols = lax.dynamic_slice_in_dim(vir_index, col_rank * col_block, col_block, 0)
    gap_rows = lookup(occ_rows, occ_energy) - lookup(vir_rows, vir_energy)
    gap_cols = lookup(occ_cols, occ_energy) - lookup(vir_cols, vir_energy)
    return accumulated + product / (gap_rows[:, None] + gap_cols[None, :])


def solution(mesh):
    in_specs = (P("row", "col"), P("row", "col"), P(("row", "col"), None), P(), P(), P(), P())
    out_specs = P("row", "col")
    return jax.shard_map(
        on_device, mesh=mesh, in_specs=in_specs, out_specs=out_specs, check_vma=False
    )
```

profile of v0, /device:TPU:11, one launch (start us, length us, event | category | flops | bytes accessed | tf_op | source)
XLA Modules:
  0.0 859.0 jit_solution(15653323680229151819)
XLA Ops:
  6.5 0.0 all-gather.3.cloned.1.call-start
  6.5 2.6 copy.10
  9.1 0.0 all-gather.3.cloned.1.call-update
  9.2 0.0 all-reduce.3.cloned.1.call-start
  9.3 76.2 %all-gather.3.cloned.1.call-done = bf16[4096,1536]{0,1:T(8,128)(2,1)} async-done(((bf16[512,1536]{0,1:T(8,128)(2,1)}), bf16[4096,1536]{0,1:T(8,128)(2,1)}) %all-gather.3.cloned.1.call-update) | async-done | bytes 12582928 | tf_op jit(solution)/shard_map/all_gather | solution.py:27
  85.4 7.7 dynamic-slice_select_fusion.1
  93.1 0.0 all-reduce.3.cloned.1.call-update
  93.1 0.0 reduce-scatter.2.cloned.1.call-start
  93.2 220.5 %all-reduce.3.cloned.1.call-done = bf16[2048,1536]{0,1:T(8,128)(2,1)} async-done(((bf16[2048,1536]{0,1:T(8,128)(2,1)}), bf16[2048,1536]{0,1:T(8,128)(2,1)}) %all-reduce.3.cloned.1.call-update) | async-done | bytes 6291472 | tf_op jit(solution)/shard_map/psum | solution.py:9
  313.7 33.8 %convolution_bitcast_fusion = f32[4096,1536]{0,1:T(8,128)} fusion(bf16[2048,1536]{0,1:T(8,128)(2,1)} %all-reduce.3.cloned.1.call-done, bf16[4096,2048]{1,0:T(8,128)(2,1)} %param.7), kind=kOutput, calls=%fused_computation.1 | convolution fusion | flops 25769803776 | bytes 48234496 | tf_op jit(solution)/shard_map/dot_general | solution.py:31
  347.5 0.0 reduce-scatter.2.cloned.1.call-update
  347.5 0.0 all-gather.5.cloned.1.call-start
  347.6 157.8 %reduce-scatter.2.cloned.1.call-done = f32[512,1536]{0,1:T(8,128)} async-done(((f32[4096,1536]{0,1:T(8,128)}), f32[512,1536]{0,1:T(8,128)}) %reduce-scatter.2.cloned.1.call-update) | async-done | bytes 3145744 | tf_op jit(solution)/shard_map/reduce_scatter | solution.py:30
  505.4 0.0 copy-done
  505.4 3.6 add_convert_fusion
  508.9 0.0 all-gather.5.cloned.1.call-update
  509.0 0.2 all-reduce.5.cloned.1.call-start
  509.2 75.0 %all-gather.5.cloned.1.call-done = bf16[4096,1536]{0,1:T(8,128)(2,1)} async-done(((bf16[512,1536]{0,1:T(8,128)(2,1)}), bf16[4096,1536]{0,1:T(8,128)(2,1)}) %all-gather.5.cloned.1.call-update) | async-done | bytes 12582928 | tf_op jit(solution)/shard_map/all_gather | solution.py:37
  584.2 7.7 dynamic-slice_select_fusion
  591.9 0.0 all-reduce.5.cloned.1.call-update
  591.9 0.7 dynamic_slice.22
  592.6 0.7 dynamic_slice.23
  593.3 0.7 dynamic_slice.20
  594.1 0.7 dynamic_slice.21
  594.8 0.0 copy-done.2
  594.8 0.2 select_reduce_fusion.3
  594.9 0.0 copy-done.1
  594.9 0.7 select_reduce_fusion.1
  595.7 0.2 select_reduce_fusion.2
  595.9 1.3 select_reduce_fusion
  597.3 215.2 %all-reduce.5.cloned.1.call-done = bf16[2048,1536]{0,1:T(8,128)(2,1)} async-done(((bf16[2048,1536]{0,1:T(8,128)(2,1)}), bf16[2048,1536]{0,1:T(8,128)(2,1)}) %all-reduce.5.cloned.1.call-update) | async-done | bytes 6291472 | tf_op jit(solution)/shard_map/psum | solution.py:9
  812.5 40.0 %divide_add_fusion = f32[4096,2048]{1,0:T(8,128)} fusion(f32[4096,2048]{1,0:T(8,128)} %param.8, f32[2048]{0:T(1024)S(1)} %sub.20, f32[4096]{0:T(1024)S(1)} %sub.19, bf16[4096,1536]{0,1:T(8,128)(2,1)} %all-gather.5.cloned.1.call-done, bf16[2048,1536]{0,1:T(8,128)(2,1)} %all-reduce.5.cloned.1.call-done), kind=kOutput, calls=%fused_computation | convolution fusion | flops 25794969600 | bytes 86007808 | tf_op jit(solution)/shard_map/dot_general | solution.py:40
  (5 shorter events, 0.0 us)
Async XLA Ops:
  6.5 78.9 %all-gather.3.cloned.1.call-start = ((), (), s32[]{:S(2)}) async-start(), calls=%async_computation.1 | async-start | bytes 14155776 | tf_op jit(solution)/shard_map/all_gather | solution.py:27
  9.2 304.5 %all-reduce.3.cloned.1.call-start = ((), (), s32[]{:S(2)}) async-start(), calls=%async_computation.2 | async-start | bytes 12582912 | tf_op jit(solution)/shard_map/psum | solution.py:9
  93.1 412.2 %reduce-scatter.2.cloned.1.call-start = ((), (), s32[]{:S(2)}) async-start(), calls=%async_computation.3 | async-start | bytes 28311552 | tf_op jit(solution)/shard_map/reduce_scatter | solution.py:30
  347.5 157.9 %copy-start = (bf16[512,1536]{0,1:T(8,128)(2,1)S(1)}, bf16[512,1536]{0,1:T(8,128)(2,1)}, u32[]{:S(2)}) copy-start(bf16[512,1536]{0,1:T(8,128)(2,1)} %copy.10) | copy-start | bytes 4718596
  347.5 236.7 %all-gather.5.cloned.1.call-start = ((), (), s32[]{:S(2)}) async-start(), calls=%async_computation.4 | async-start | bytes 14155776 | tf_op jit(solution)/shard_map/all_gather | solution.py:37
  509.0 303.5 %all-reduce.5.cloned.1.call-start = ((), (), s32[]{:S(2)}) async-start(), calls=%async_computation.5 | async-start | bytes 12582912 | tf_op jit(solution)/shard_map/psum | solution.py:9
  591.9 2.9 copy-start.2
  591.9 3.0 copy-start.1
Sparse Core Ops, SparseCore 0:
  9.3 76.0 all-gather.2
  93.3 220.3 all-reduce.2
  347.6 157.6 reduce-scatter.1
  509.1 75.0 all-gather.4
  592.0 220.3 all-reduce.4
where the time goes:
time: 863 us; the launch traced here: 859 us
  waiting for transfers between devices  745 us (86%)
  matrix products  73.8 us (9%)
  other arithmetic  21.4 us (2%)
  between operations  13.2 us (2%)
    psum x2, waiting for transfers between devices, spread(): return lax.psum(kept, axis)  436 us
    reduce_scatter x1, waiting for transfers between devices, on_device(): lax.psum_scatter(jnp.dot(amplitudes, b_cols, preferred_element_type=jnp.f...  158 us
    all_gather x1, waiting for transfers between devices, on_device(): b_rows = lax.all_gather(cholesky, 'col', axis=0, tiled=True)  76.2 us
    all_gather x1, waiting for transfers between devices, on_device(): x_rows = lax.all_gather(x_piece, 'col', axis=0, tiled=True)  75 us
    dot_general x1, matrix products, on_device(): lax.dot_general(x_rows, x_cols, (((1,), (1,)), ((), ())), preferred_eleme...  40 us
    dot_general x1, matrix products, on_device(): jnp.dot(amplitudes, b_cols, preferred_element_type=jnp.float32)  33.8 us
  transfers between devices with their start and end apart: 5, of which 5 were waited for; matrix products, arithmetic and copies ran while one was open for 1% of the time, Pallas kernels for 0%

commit v1 on v0

v1 whole, which is shorter than its diff:
```python
import jax
import jax.numpy as jnp
from jax import lax
from jax.sharding import PartitionSpec as P


def lookup(index, table):
    hits = index[:, None] == jnp.arange(table.shape[0], dtype=jnp.int32)[None, :]
    return jnp.sum(jnp.where(hits, table[None, :], jnp.zeros((), table.dtype)), axis=1)


def chunk_bounds(width):
    count = 3 if width % 384 == 0 else 1
    step = width // count
    return [(at * step, step) for at in range(count)]


def after(value, *earlier):
    return lax.optimization_barrier((value, *earlier))[0]


def along_rows(piece, row_count):
    held = [piece]
    for shift in range(1, row_count):
        pairs = [(r, (r + shift) % row_count) for r in range(row_count)]
        held.append(lax.ppermute(piece, "row", pairs))
    return held


def to_columns(held, row_count, col_count):
    ratio = col_count // row_count
    row_rank = lax.axis_index("row")
    col_rank = lax.axis_index("col")
    size, width = held[0].shape
    out = jnp.zeros((row_count * size, width), held[0].dtype)
    for turn in range(row_count):
        wanted = (col_rank % row_count - turn) % row_count
        send = lax.select_n((row_rank - wanted) % row_count, *held)
        pairs = [
            ((c % ratio) * row_count + (c // ratio + turn) % row_count, c)
            for c in range(col_count)
        ]
        got = lax.ppermute(send, "col", pairs)
        place = (col_rank // ratio + turn) % row_count
        out = lax.dynamic_update_slice_in_dim(out, got, place * size, 0)
    return out


def on_device(amplitudes, accumulated, cholesky, occ_index, vir_index, occ_energy, vir_energy):
    row_count = lax.axis_size("row")
    col_count = lax.axis_size("col")
    row_rank = lax.axis_index("row")
    col_rank = lax.axis_index("col")
    row_block = amplitudes.shape[0]
    col_block = amplitudes.shape[1]
    size = cholesky.shape[0]

    upward = [1 << bit for bit in range(1, col_count.bit_length() - 1)]
    downward = upward[::-1]
    levels = len(upward)
    even = col_rank % 2 == 0

    def block_of(base, from_up, slot):
        mask = 0
        for level in range(levels):
            if slot >> (levels - 1 - level) & 1:
                mask = mask + jnp.where(from_up, upward[level], downward[level])
        return base ^ mask

    def rows_of(block):
        return lax.dynamic_slice_in_dim(amplitudes, block * size, size, 0)

    slots = range(1 << levels)
    half = len(slots) // 2
    other = col_rank ^ 1
    t_send = jnp.concatenate([rows_of(block_of(other, ~even, s)) for s in slots], 0)
    t_pass = jnp.concatenate([rows_of(block_of(col_rank, even, s)) for s in slots[half:]], 0)
    t_keep = jnp.concatenate([rows_of(block_of(col_rank, even, s)) for s in slots[:half]], 0)
    core_pairs = [(c, c ^ 1) for c in range(col_count)]

    def sums(b_part, at_core, at_last):
        def dot(rows):
            return jnp.dot(rows, b_part, preferred_element_type=jnp.float32)

        came = lax.ppermute(dot(t_send), "col", core_pairs)
        came = after(came, *at_core)
        b_part = after(b_part, came)
        send = dot(t_pass) + came[half * size :]
        total = dot(t_keep) + came[: half * size]
        for level in range(levels):
            if level > 0:
                middle = total.shape[0] // 2
                send, total = total[middle:], total[:middle]
            pairs = [
                (c, c ^ (upward[level] if c % 2 == 0 else downward[level]))
                for c in range(col_count)
            ]
            if level == levels - 1:
                send = after(send, *at_last)
            total = total + lax.ppermute(send, "col", pairs)
        return total, came

    occ_rows = lax.dynamic_slice_in_dim(occ_index, row_rank * row_block, row_block, 0)
    vir_rows = lax.dynamic_slice_in_dim(vir_index, row_rank * row_block, row_block, 0)
    occ_cols = lax.dynamic_slice_in_dim(occ_index, col_rank * col_block, col_block, 0)
    vir_cols = lax.dynamic_slice_in_dim(vir_index, col_rank * col_block, col_block, 0)
    gap_rows = lookup(occ_rows, occ_energy) - lookup(vir_rows, vir_energy)
    gap_cols = lookup(occ_cols, occ_energy) - lookup(vir_cols, vir_energy)

    chols, b_held = [], []
    for start, width in chunk_bounds(cholesky.shape[1]):
        chol = cholesky[:, start : start + width]
        chols.append(chol)
        first = after(chol, *b_held[-1]) if b_held else chol
        b_held.append(along_rows(first, row_count))

    came, x_held, x_rows, x_cols = None, [], [], []
    for at, chol in enumerate(chols):
        held = b_held[at]
        if at > 0:
            held = lax.optimization_barrier((*held, came))[: len(held)]
        b_cols = to_columns(held, row_count, col_count)
        if at > 0:
            b_cols = after(b_cols, x_held[-1][0])
        elif len(chols) > 1:
            b_cols = after(b_cols, *b_held[1])
        beside = x_held[-1] if at > 0 else b_held[min(2, len(chols) - 1)]
        at_last = beside[2:] + (x_rows[-1:] if at > 0 else [])
        summed, came = sums(b_cols, beside[1:2], at_last)
        x_piece = (chol.astype(jnp.float32) + summed).astype(jnp.bfloat16)
        if at > 1:
            x_piece = after(x_piece, x_cols[at - 2])
        x_rows.append(lax.all_gather(x_piece, "col", axis=0, tiled=True))
        x_held.append(along_rows(x_piece, row_count))
        x_cols.append(to_columns(x_held[-1], row_count, col_count))

    product = None
    for rows, cols in zip(x_rows, x_cols):
        term = lax.dot_general(
            rows, cols, (((1,), (1,)), ((), ())), preferred_element_type=jnp.float32
        )
        product = term if product is None else product + term
    return accumulated + product / (gap_rows[:, None] + gap_cols[None, :])


def solution(mesh):
    in_specs = (P("row", "col"), P("row", "col"), P(("row", "col"), None), P(), P(), P(), P())
    out_specs = P("row", "col")
    return jax.shard_map(
        on_device, mesh=mesh, in_specs=in_specs, out_specs=out_specs, check_vma=False
    )
```

time: 863 us -> 605 us (0.70)
  waiting for transfers between devices: 745 us -> 296 us
  starting transfers between devices: 0.35 us -> 84.3 us
  matrix products: 73.8 us -> 132 us
  local copies, waits for them, and re-layouts: 5.46 us -> 47.6 us
    psum x2 -> x0, waiting for transfers between devices: 436 us -> none  [spread(): return lax.psum(kept, axis)]
    ppermute x0 -> x51, waiting for transfers between devices: none -> 296 us  [the longest x18 124 us: along_rows(): held.append(lax.ppermute(piece, 'row', pairs))]
    reduce_scatter x1 -> x0, waiting for transfers between devices: 158 us -> none  [on_device(): lax.psum_scatter(jnp.dot(amplitudes, b_cols, preferred_element_type=jnp.f...]
    all_gather x2 -> x3, waiting for transfers between devices: 151 us -> 0.01 us  [on_device(): x_rows.append(lax.all_gather(x_piece, 'col', axis=0, tiled=True))]
    ppermute x0 -> x51, starting transfers between devices: none -> 84.2 us  [the longest x24 57.6 us: to_columns(): got = lax.ppermute(send, 'col', pairs)]
    dot_general x2 -> x12, matrix products: 73.8 us -> 132 us  [the longest x3 79.5 us: on_device(): lax.dot_general(rows, cols, (((1,), (1,)), ((), ())), preferred_element_t...]
    dynamic_update_slice x0 -> x24, local copies, waits for them, and re-layouts: none -> 18.6 us  [to_columns(): out = lax.dynamic_update_slice_in_dim(out, got, place * size, 0)]
    dynamic_slice x0 -> x1, local copies, waits for them, and re-layouts: none -> 12.4 us  [rows_of(): return lax.dynamic_slice_in_dim(amplitudes, block * size, size, 0)]
  transfers between devices with their start and end apart: 5 -> 54, of which waited for: 5 -> 26; matrix products, arithmetic and copies ran while one was open for 1% -> 18% of each run, Pallas kernels for 0% -> 0%
where the time goes in v1:
time: 605 us; the launch traced here: 595 us
  waiting for transfers between devices  296 us (49%)
  matrix products  132 us (22%)
  starting transfers between devices  84.3 us (14%)
  local copies, waits for them, and re-layouts  47.6 us (8%)
  other arithmetic  21.3 us (4%)
  between operations  14.5 us (2%)
    ppermute x18, waiting for transfers between devices, along_rows(): held.append(lax.ppermute(piece, 'row', pairs))  124 us
    ppermute x24, waiting for transfers between devices, to_columns(): got = lax.ppermute(send, 'col', pairs)  91.1 us
    ppermute x6, waiting for transfers between devices, sums(): total = total + lax.ppermute(send, 'col', pairs)  80.5 us
    dot_general x3, matrix products, on_device(): lax.dot_general(rows, cols, (((1,), (1,)), ((), ())), preferred_element_t...  79.5 us
    ppermute x24, starting transfers between devices, to_columns(): got = lax.ppermute(send, 'col', pairs)  57.6 us
    dot_general x9, matrix products, dot(): return jnp.dot(rows, b_part, preferred_element_type=jnp.float32)  52.1 us
    dynamic_update_slice x24, local copies, waits for them, and re-layouts, to_columns(): out = lax.dynamic_update_slice_in_dim(out, got, place * size, 0)  18.6 us
    ppermute x18, starting transfers between devices, along_rows(): held.append(lax.ppermute(piece, 'row', pairs))  15.5 us
  transfers between devices with their start and end apart: 54, of which 26 were waited for; matrix products, arithmetic and copies ran while one was open for 18% of the time, Pallas kernels for 0%

profile of v1, /device:TPU:11, one launch (start us, length us, event | category | flops | bytes accessed | tf_op | source)
XLA Modules:
  0.0 595.2 jit_solution(881629851054940284)
XLA Ops:
  12.7 9.2 %collective-permute-done = bf16[512,512]{1,0:T(8,128)(2,1)S(1)} collective-permute-done((bf16[512,512]{1,0:T(8,128)(2,1)}, bf16[512,512]{1,0:T(8,128)(2,1)S(1)}, u32[]{:S(2)}, u32[]{:S(2)}) %collective-permute-start) | collective-permute-done | bytes 524320 | tf_op jit(solution)/shard_map/ppermute | solution.py:26
  21.9 32.9 %collective-permute-done.1 = bf16[512,512]{1,0:T(8,128)(2,1)} collective-permute-done((bf16[512,512]{1,0:T(8,128)(2,1)}, bf16[512,512]{1,0:T(8,128)(2,1)}, u32[]{:S(2)}, u32[]{:S(2)}) %collective-permute-start.1) | collective-permute-done | bytes 524320 | tf_op jit(solution)/shard_map/ppermute | solution.py:26
  75.3 4.8 collective-permute-done.4
  82.0 12.4 %constant_dynamic-slice_fusion.7 = (bf16[512,2048]{1,0:T(8,128)(2,1)}, bf16[512,2048]{1,0:T(8,128)(2,1)}, bf16[512,2048]{1,0:T(8,128)(2,1)}, bf16[512,2048]{1,0:...) fusion(bf16[4096,2048]{1,0:T(8,128)(2,1)} %param.7, ...), kind=kLoop, calls=%fused_computation.88 | loop fusion | bytes 33554464 | tf_op jit(solution)/shard_map/dynamic_slice | solution.py:71
  99.8 7.8 %collective-permute-done.8 = bf16[512,512]{1,0:T(8,128)(2,1)} collective-permute-done((bf16[512,512]{1,0:T(8,128)(2,1)S(1)}, bf16[512,512]{1,0:T(8,128)(2,1)}, u32[]{:S(2)}, u32[]{:S(2)}) %collective-permute-start.8) | collective-permute-done | bytes 524320 | tf_op jit(solution)/shard_map/ppermute | solution.py:26
  107.6 5.9 collective-permute-done.9
  113.5 6.3 %fusion.20 = f32[2048,512]{1,0:T(8,128)S(1)} fusion(bf16[2048,512]{1,0:T(8,128)(2,1)S(1)} %constant_dynamic-update-slice_fusion.20, bf16[512,2048]{1,0:T(8,128)(2,1)S(1)} %copy-done.16, bf16[512,2048]{1,0:T(8,128)(2,1)S(1)} %copy-done.17, bf16[512,2048]{1,0:T(8,128)(2,1)S(1)} %copy-done.18, bf16[512,2048]{1,0:T(8,128)(2,1)} %get-tuple-element.55), kind=kOutput, calls=%fused_computation.97 | convolution fusion | flops 4328521728 | bytes 14680064 | tf_op jit(solution)/shard_map/dot_general | solution.py:83
  120.3 13.5 %collective-permute-done.11 = bf16[512,512]{1,0:T(8,128)(2,1)S(1)} collective-permute-done((bf16[512,512]{1,0:T(8,128)(2,1)S(1)}, bf16[512,512]{1,0:T(8,128)(2,1)S(1)}, u32[]{:S(2)}, u32[]{:S(2)}) %collective-permute-start.11) | collective-permute-done | bytes 524320 | tf_op jit(solution)/shard_map/ppermute | solution.py:26
  142.6 20.1 %collective-permute-done.12 = f32[1024,512]{1,0:T(8,128)S(1)} collective-permute-done((f32[1024,512]{1,0:T(8,128)S(1)}, f32[1024,512]{1,0:T(8,128)S(1)}, u32[]{:S(2)}, u32[]{:S(2)}) %collective-permute-start.12) | collective-permute-done | bytes 2097184 | tf_op jit(solution)/shard_map/ppermute | solution.py:100
  163.5 8.5 %collective-permute-done.13 = bf16[512,512]{1,0:T(8,128)(2,1)S(1)} collective-permute-done((bf16[512,512]{1,0:T(8,128)(2,1)S(1)}, bf16[512,512]{1,0:T(8,128)(2,1)S(1)}, u32[]{:S(2)}, u32[]{:S(2)}) %collective-permute-start.13) | collective-permute-done | bytes 524320 | tf_op jit(solution)/shard_map/ppermute | solution.py:26
  187.4 18.3 %collective-permute-done.23 = bf16[512,512]{1,0:T(8,128)(2,1)S(1)} collective-permute-done((bf16[512,512]{1,0:T(8,128)(2,1)S(1)}, bf16[512,512]{1,0:T(8,128)(2,1)S(1)}, u32[]{:S(2)}, u32[]{:S(2)}) %collective-permute-start.23) | collective-permute-done | bytes 524320 | tf_op jit(solution)/shard_map/ppermute | solution.py:43
  208.0 4.2 collective-permute-done.24
  215.8 10.9 %fusion.19 = f32[2048,512]{1,0:T(8,128)} fusion(bf16[2048,512]{1,0:T(8,128)(2,1)} %constant_dynamic-update-slice_fusion.12, bf16[512,2048]{1,0:T(8,128)(2,1)} %get-tuple-element.52, bf16[512,2048]{1,0:T(8,128)(2,1)} %get-tuple-element.53, bf16[512,2048]{1,0:T(8,128)(2,1)} %get-tuple-element.54, bf16[512,2048]{1,0:T(8,128)(2,1)} %get-tuple-element.55), kind=kOutput, calls=%fused_computation.96 | convolution fusion | flops 4328521728 | bytes 14680064 | tf_op jit(solution)/shard_map/dot_general | solution.py:83
  226.8 13.1 %collective-permute-done.16 = bf16[512,512]{1,0:T(8,128)(2,1)S(1)} collective-permute-done((bf16[512,512]{1,0:T(8,128)(2,1)S(1)}, bf16[512,512]{1,0:T(8,128)(2,1)S(1)}, u32[]{:S(2)}, u32[]{:S(2)}) %collective-permute-start.16) | collective-permute-done | bytes 524320 | tf_op jit(solution)/shard_map/ppermute | solution.py:26
  239.9 5.8 slice_add_fusion.1
  247.6 3.9 fusion.4
  251.5 30.7 %collective-permute-done.28 = f32[1024,512]{1,0:T(8,128)S(1)} collective-permute-done((f32[1024,512]{1,0:T(8,128)S(1)}, f32[1024,512]{1,0:T(8,128)S(1)}, u32[]{:S(2)}, u32[]{:S(2)}) %collective-permute-start.28) | collective-permute-done | bytes 2097184 | tf_op jit(solution)/shard_map/ppermute | solution.py:100
  300.3 18.3 %collective-permute-done.37 = bf16[512,512]{1,0:T(8,128)(2,1)S(1)} collective-permute-done((bf16[512,512]{1,0:T(8,128)(2,1)S(1)}, bf16[512,512]{1,0:T(8,128)(2,1)S(1)}, u32[]{:S(2)}, u32[]{:S(2)}) %collective-permute-start.37) | collective-permute-done | bytes 524320 | tf_op jit(solution)/shard_map/ppermute | solution.py:43
  320.9 5.5 collective-permute-done.38
  330.1 10.8 %fusion.18 = f32[2048,512]{1,0:T(8,128)} fusion(bf16[2048,512]{1,0:T(8,128)(2,1)} %constant_dynamic-update-slice_fusion.4, bf16[512,2048]{1,0:T(8,128)(2,1)} %get-tuple-element.52, bf16[512,2048]{1,0:T(8,128)(2,1)} %get-tuple-element.53, bf16[512,2048]{1,0:T(8,128)(2,1)} %get-tuple-element.54, bf16[512,2048]{1,0:T(8,128)(2,1)} %get-tuple-element.55), kind=kOutput, calls=%fused_computation.95 | convolution fusion | flops 4328521728 | bytes 14680064 | tf_op jit(solution)/shard_map/dot_general | solution.py:83
  341.3 12.9 %collective-permute-done.30 = bf16[512,512]{1,0:T(8,128)(2,1)S(1)} collective-permute-done((bf16[512,512]{1,0:T(8,128)(2,1)S(1)}, bf16[512,512]{1,0:T(8,128)(2,1)S(1)}, u32[]{:S(2)}, u32[]{:S(2)}) %collective-permute-start.30) | collective-permute-done | bytes 524320 | tf_op jit(solution)/shard_map/ppermute | solution.py:26
  355.0 5.8 slice_add_fusion
  363.6 4.0 fusion.3
  367.7 29.7 %collective-permute-done.42 = f32[1024,512]{1,0:T(8,128)S(1)} collective-permute-done((f32[1024,512]{1,0:T(8,128)S(1)}, f32[1024,512]{1,0:T(8,128)S(1)}, u32[]{:S(2)}, u32[]{:S(2)}) %collective-permute-start.42) | collective-permute-done | bytes 2097184 | tf_op jit(solution)/shard_map/ppermute | solution.py:100
  415.7 18.4 %collective-permute-done.19 = bf16[512,512]{1,0:T(8,128)(2,1)S(1)} collective-permute-done((bf16[512,512]{1,0:T(8,128)(2,1)S(1)}, bf16[512,512]{1,0:T(8,128)(2,1)S(1)}, u32[]{:S(2)}, u32[]{:S(2)}) %collective-permute-start.19) | collective-permute-done | bytes 524320 | tf_op jit(solution)/shard_map/ppermute | solution.py:43
  436.4 5.7 collective-permute-done.20
  450.3 6.8 %collective-permute-start.34 = (bf16[512,512]{1,0:T(8,128)(2,1)}, bf16[512,512]{1,0:T(8,128)(2,1)S(1)}, u32[]{:S(2)}, u32[]{:S(2)}) collective-permute-start(bf16[512,512]{1,0:T(8,128)(2,1)} %get-tuple-element.65), channel_id=1, source_target_pairs={{1,0},{5,1},{2,2},{6,3},{3,4},{7,5},{0,6},{4,7},{9,8},{13,9},{10,1... | collective-permute-start | bytes 1572872 | tf_op jit(solution)/shard_map/ppermute | solution.py:43
  465.8 9.8 %collective-permute-done.34 = bf16[512,512]{1,0:T(8,128)(2,1)S(1)} collective-permute-done((bf16[512,512]{1,0:T(8,128)(2,1)}, bf16[512,512]{1,0:T(8,128)(2,1)S(1)}, u32[]{:S(2)}, u32[]{:S(2)}) %collective-permute-start.34) | collective-permute-done | bytes 524320 | tf_op jit(solution)/shard_map/ppermute | solution.py:43
  475.8 18.8 %fusion.22 = f32[4096,2048]{1,0:T(8,128)} fusion(bf16[4096,512]{1,0:T(8,128)(2,1)} %all-gather.4.cloned.1.call-done, bf16[2048,512]{1,0:T(8,128)(2,1)} %constant_dynamic-update-slice_fusion.16), kind=kOutput, calls=%fused_computation.99 | convolution fusion | flops 8589934592 | bytes 39845888 | tf_op jit(solution)/shard_map/dot_general | solution.py:139
  495.0 13.7 %collective-permute-done.45 = bf16[512,512]{1,0:T(8,128)(2,1)S(1)} collective-permute-done((bf16[512,512]{1,0:T(8,128)(2,1)S(1)}, bf16[512,512]{1,0:T(8,128)(2,1)S(1)}, u32[]{:S(2)}, u32[]{:S(2)}) %collective-permute-start.45) | collective-permute-done | bytes 524320 | tf_op jit(solution)/shard_map/ppermute | solution.py:26
  519.6 14.4 %fusion.23 = f32[4096,2048]{1,0:T(8,128)} fusion(bf16[4096,512]{1,0:T(8,128)(2,1)S(1)} %copy-done.31, bf16[2048,512]{1,0:T(8,128)(2,1)S(1)} %constant_dynamic-update-slice_fusion.8), kind=kOutput, calls=%fused_computation.100 | convolution fusion | flops 8589934592 | bytes 39845888 | tf_op jit(solution)/shard_map/dot_general | solution.py:139
  541.9 46.3 %divide_add_fusion = f32[4096,2048]{1,0:T(8,128)} fusion(f32[4096,2048]{1,0:T(8,128)} %param.8, f32[4096,2048]{1,0:T(8,128)} %fusion.22, f32[4096,2048]{1,0:T(8,128)} %fusion.23, f32[2048]{0:T(1024)S(1)} %sub.106, f32[4096]{0:T(1024)S(1)} %sub.105, bf16[4096,512]{1,0:T(8,128)(2,1)} %all-gather.8.cloned.1.call-done, ...), kind=kOutput, calls=%fused_computation | convolution fusion | flops 8631877632 | bytes 140533760 | tf_op jit(solution)/shard_map/dot_general | solution.py:139
  (214 shorter events, 151.7 us)
Async XLA Ops:
  6.5 281.2 %all-gather.4.cloned.1.call-start = ((), (), s32[]{:S(2)}) async-start(), calls=%async_computation | async-start | bytes 4718592 | tf_op jit(solution)/shard_map/all_gather | solution.py:133
  10.2 44.6 %collective-permute-start.1 = (bf16[512,512]{1,0:T(8,128)(2,1)}, bf16[512,512]{1,0:T(8,128)(2,1)}, u32[]{:S(2)}, u32[]{:S(2)}) collective-permute-start(bf16[512,512]{1,0:T(8,128)(2,1)} %get-tuple-element.83), channel_id=1, source_target_pairs={{0,16},{8,24},{16,0},{24,8},{1,17},{9,25},{17,1},{25,9},{2,18},{10... | collective-permute-start | bytes 1572872 | tf_op jit(solution)/shard_map/ppermute | solution.py:26
  11.2 46.4 %collective-permute-start.2 = (bf16[512,512]{1,0:T(8,128)(2,1)}, bf16[512,512]{1,0:T(8,128)(2,1)}, u32[]{:S(2)}, u32[]{:S(2)}) collective-permute-start(bf16[512,512]{1,0:T(8,128)(2,1)} %get-tuple-element.83), channel_id=1, source_target_pairs={{0,24},{8,0},{16,8},{24,16},{1,25},{9,1},{17,9},{25,17},{2,26},{10... | collective-permute-start | bytes 1572872 | tf_op jit(solution)/shard_map/ppermute | solution.py:26
  65.9 33.9 %collective-permute-start.7 = (bf16[512,512]{1,0:T(8,128)(2,1)S(1)}, bf16[512,512]{1,0:T(8,128)(2,1)}, u32[]{:S(2)}, u32[]{:S(2)}) collective-permute-start(bf16[512,512]{1,0:T(8,128)(2,1)S(1)} %get-tuple-element.34), channel_id=1, source_target_pairs={{0,8},{8,16},{16,24},{24,0},{1,9},{9,17},{17,25},{25,1},{2,10},{10... | collective-permute-start | bytes 1572872 | tf_op jit(solution)/shard_map/ppermute | solution.py:26
  66.0 41.6 %collective-permute-start.8 = (bf16[512,512]{1,0:T(8,128)(2,1)S(1)}, bf16[512,512]{1,0:T(8,128)(2,1)}, u32[]{:S(2)}, u32[]{:S(2)}) collective-permute-start(bf16[512,512]{1,0:T(8,128)(2,1)S(1)} %get-tuple-element.34), channel_id=1, source_target_pairs={{0,16},{8,24},{16,0},{24,8},{1,17},{9,25},{17,1},{25,9},{2,18},{10... | collective-permute-start | bytes 1572872 | tf_op jit(solution)/shard_map/ppermute | solution.py:26
  67.3 46.2 %collective-permute-start.9 = (bf16[512,512]{1,0:T(8,128)(2,1)S(1)}, bf16[512,512]{1,0:T(8,128)(2,1)}, u32[]{:S(2)}, u32[]{:S(2)}) collective-permute-start(bf16[512,512]{1,0:T(8,128)(2,1)S(1)} %get-tuple-element.34), channel_id=1, source_target_pairs={{0,24},{8,0},{16,8},{24,16},{1,25},{9,1},{17,9},{25,17},{2,26},{10... | collective-permute-start | bytes 1572872 | tf_op jit(solution)/shard_map/ppermute | solution.py:26
  139.0 33.0 %collective-permute-start.13 = (bf16[512,512]{1,0:T(8,128)(2,1)S(1)}, bf16[512,512]{1,0:T(8,128)(2,1)S(1)}, u32[]{:S(2)}, u32[]{:S(2)}) collective-permute-start(bf16[512,512]{1,0:T(8,128)(2,1)S(1)} %get-tuple-element.42), channel_id=1, source_target_pairs={{0,16},{8,24},{16,0},{24,8},{1,17},{9,25},{17,1},{25,9},{2,18},{10... | collective-permute-start | bytes 1572872 | tf_op jit(solution)/shard_map/ppermute | solution.py:26
  139.0 34.9 %collective-permute-start.14 = (bf16[512,512]{1,0:T(8,128)(2,1)S(1)}, bf16[512,512]{1,0:T(8,128)(2,1)S(1)}, u32[]{:S(2)}, u32[]{:S(2)}) collective-permute-start(bf16[512,512]{1,0:T(8,128)(2,1)S(1)} %get-tuple-element.42), channel_id=1, source_target_pairs={{0,24},{8,0},{16,8},{24,16},{1,25},{9,1},{17,9},{25,17},{2,26},{10... | collective-permute-start | bytes 1572872 | tf_op jit(solution)/shard_map/ppermute | solution.py:26
  173.9 40.8 %collective-permute-start.15 = (f32[512,512]{1,0:T(8,128)S(1)}, f32[512,512]{1,0:T(8,128)S(1)}, u32[]{:S(2)}, u32[]{:S(2)}) collective-permute-start(f32[512,512]{1,0:T(8,128)S(1)} %slice.61), channel_id=1, source_target_pairs={{0,4},{1,3},{2,6},{3,1},{4,0},{5,7},{6,2},{7,5},{8,12},{9,11},{10,... | collective-permute-start | bytes 3145736 | tf_op jit(solution)/shard_map/ppermute | solution.py:100
  180.7 31.4 %collective-permute-start.24 = (bf16[512,512]{1,0:T(8,128)(2,1)S(1)}, bf16[512,512]{1,0:T(8,128)(2,1)S(1)}, u32[]{:S(2)}, u32[]{:S(2)}) collective-permute-start(bf16[512,512]{1,0:T(8,128)(2,1)S(1)} %get-tuple-element.81), channel_id=1, source_target_pairs={{1,0},{5,1},{2,2},{6,3},{3,4},{7,5},{0,6},{4,7},{9,8},{13,9},{10,1... | collective-permute-start | bytes 1572872 | tf_op jit(solution)/shard_map/ppermute | solution.py:43
  184.0 29.8 %collective-permute-start.26 = (bf16[512,512]{1,0:T(8,128)(2,1)S(1)}, bf16[512,512]{1,0:T(8,128)(2,1)S(1)}, u32[]{:S(2)}, u32[]{:S(2)}) collective-permute-start(bf16[512,512]{1,0:T(8,128)(2,1)S(1)} %get-tuple-element.79), channel_id=1, source_target_pairs={{3,0},{7,1},{0,2},{4,3},{1,4},{5,5},{2,6},{6,7},{11,8},{15,9},{8,1... | collective-permute-start | bytes 1572872 | tf_op jit(solution)/shard_map/ppermute | solution.py:43
  226.7 176.3 %all-gather.6.cloned.1.call-start = ((), (), s32[]{:S(2)}) async-start(), calls=%async_computation.1 | async-start | bytes 4718592 | tf_op jit(solution)/shard_map/all_gather | solution.py:133
  245.7 36.6 %collective-permute-start.28 = (f32[1024,512]{1,0:T(8,128)S(1)}, f32[1024,512]{1,0:T(8,128)S(1)}, u32[]{:S(2)}, u32[]{:S(2)}) collective-permute-start(f32[1024,512]{1,0:T(8,128)S(1)} %slice_add_fusion.1), channel_id=1, source_target_pairs={{0,2},{1,5},{2,0},{3,7},{4,6},{5,1},{6,4},{7,3},{8,10},{9,13},{10,... | collective-permute-start | bytes 6291464 | tf_op jit(solution)/shard_map/ppermute | solution.py:100
  245.9 41.0 %collective-permute-start.17 = (bf16[512,512]{1,0:T(8,128)(2,1)S(1)}, bf16[512,512]{1,0:T(8,128)(2,1)S(1)}, u32[]{:S(2)}, u32[]{:S(2)}) collective-permute-start(bf16[512,512]{1,0:T(8,128)(2,1)S(1)} %copy-done.5), channel_id=1, source_target_pairs={{0,16},{8,24},{16,0},{24,8},{1,17},{9,25},{17,1},{25,9},{2,18},{10... | collective-permute-start | bytes 1572872 | tf_op jit(solution)/shard_map/ppermute | solution.py:26
  247.6 40.2 %collective-permute-start.18 = (bf16[512,512]{1,0:T(8,128)(2,1)S(1)}, bf16[512,512]{1,0:T(8,128)(2,1)}, u32[]{:S(2)}, u32[]{:S(2)}) collective-permute-start(bf16[512,512]{1,0:T(8,128)(2,1)S(1)} %copy-done.5), channel_id=1, source_target_pairs={{0,24},{8,0},{16,8},{24,16},{1,25},{9,1},{17,9},{25,17},{2,26},{10... | collective-permute-start | bytes 1572872 | tf_op jit(solution)/shard_map/ppermute | solution.py:26
  287.8 41.1 %collective-permute-start.29 = (f32[512,512]{1,0:T(8,128)}, f32[512,512]{1,0:T(8,128)S(1)}, u32[]{:S(2)}, u32[]{:S(2)}) collective-permute-start(f32[512,512]{1,0:T(8,128)} %slice.63), channel_id=1, source_target_pairs={{0,4},{1,3},{2,6},{3,1},{4,0},{5,7},{6,2},{7,5},{8,12},{9,11},{10,... | collective-permute-start | bytes 3145736 | tf_op jit(solution)/shard_map/ppermute | solution.py:100
  294.7 31.7 %collective-permute-start.38 = (bf16[512,512]{1,0:T(8,128)(2,1)S(1)}, bf16[512,512]{1,0:T(8,128)(2,1)S(1)}, u32[]{:S(2)}, u32[]{:S(2)}) collective-permute-start(bf16[512,512]{1,0:T(8,128)(2,1)S(1)} %get-tuple-element.77), channel_id=1, source_target_pairs={{1,0},{5,1},{2,2},{6,3},{3,4},{7,5},{0,6},{4,7},{9,8},{13,9},{10,1... | collective-permute-start | bytes 1572872 | tf_op jit(solution)/shard_map/ppermute | solution.py:43
  297.1 30.1 %collective-permute-start.39 = (bf16[512,512]{1,0:T(8,128)(2,1)S(1)}, bf16[512,512]{1,0:T(8,128)(2,1)S(1)}, u32[]{:S(2)}, u32[]{:S(2)}) collective-permute-start(bf16[512,512]{1,0:T(8,128)(2,1)S(1)} %get-tuple-element.76), channel_id=1, source_target_pairs={{2,0},{6,1},{3,2},{7,3},{0,4},{4,5},{1,6},{5,7},{10,8},{14,9},{11,... | collective-permute-start | bytes 1572872 | tf_op jit(solution)/shard_map/ppermute | solution.py:43
  297.2 30.8 %collective-permute-start.40 = (bf16[512,512]{1,0:T(8,128)(2,1)S(1)}, bf16[512,512]{1,0:T(8,128)(2,1)S(1)}, u32[]{:S(2)}, u32[]{:S(2)}) collective-permute-start(bf16[512,512]{1,0:T(8,128)(2,1)S(1)} %get-tuple-element.75), channel_id=1, source_target_pairs={{3,0},{7,1},{0,2},{4,3},{1,4},{5,5},{2,6},{6,7},{11,8},{15,9},{8,1... | collective-permute-start | bytes 1572872 | tf_op jit(solution)/shard_map/ppermute | solution.py:43
  341.0 200.9 %all-gather.8.cloned.1.call-start = ((), (), s32[]{:S(2)}) async-start(), calls=%async_computation.2 | async-start | bytes 4718592 | tf_op jit(solution)/shard_map/all_gather | solution.py:133
  360.8 36.6 %collective-permute-start.42 = (f32[1024,512]{1,0:T(8,128)S(1)}, f32[1024,512]{1,0:T(8,128)S(1)}, u32[]{:S(2)}, u32[]{:S(2)}) collective-permute-start(f32[1024,512]{1,0:T(8,128)S(1)} %slice_add_fusion), channel_id=1, source_target_pairs={{0,2},{1,5},{2,0},{3,7},{4,6},{5,1},{6,4},{7,3},{8,10},{9,13},{10,... | collective-permute-start | bytes 6291464 | tf_op jit(solution)/shard_map/ppermute | solution.py:100
  361.7 40.5 %collective-permute-start.31 = (bf16[512,512]{1,0:T(8,128)(2,1)S(1)}, bf16[512,512]{1,0:T(8,128)(2,1)S(1)}, u32[]{:S(2)}, u32[]{:S(2)}) collective-permute-start(bf16[512,512]{1,0:T(8,128)(2,1)S(1)} %copy-done.7), channel_id=1, source_target_pairs={{0,16},{8,24},{16,0},{24,8},{1,17},{9,25},{17,1},{25,9},{2,18},{10... | collective-permute-start | bytes 1572872 | tf_op jit(solution)/shard_map/ppermute | solution.py:26
  363.1 39.9 %collective-permute-start.32 = (bf16[512,512]{1,0:T(8,128)(2,1)S(1)}, bf16[512,512]{1,0:T(8,128)(2,1)}, u32[]{:S(2)}, u32[]{:S(2)}) collective-permute-start(bf16[512,512]{1,0:T(8,128)(2,1)S(1)} %copy-done.7), channel_id=1, source_target_pairs={{0,24},{8,0},{16,8},{24,16},{1,25},{9,1},{17,9},{25,17},{2,26},{10... | collective-permute-start | bytes 1572872 | tf_op jit(solution)/shard_map/ppermute | solution.py:26
  402.9 41.7 %collective-permute-start.43 = (f32[512,512]{1,0:T(8,128)}, f32[512,512]{1,0:T(8,128)S(1)}, u32[]{:S(2)}, u32[]{:S(2)}) collective-permute-start(f32[512,512]{1,0:T(8,128)} %slice.65), channel_id=1, source_target_pairs={{0,4},{1,3},{2,6},{3,1},{4,0},{5,7},{6,2},{7,5},{8,12},{9,11},{10,... | collective-permute-start | bytes 3145736 | tf_op jit(solution)/shard_map/ppermute | solution.py:100
  410.3 31.8 %collective-permute-start.20 = (bf16[512,512]{1,0:T(8,128)(2,1)S(1)}, bf16[512,512]{1,0:T(8,128)(2,1)S(1)}, u32[]{:S(2)}, u32[]{:S(2)}) collective-permute-start(bf16[512,512]{1,0:T(8,128)(2,1)S(1)} %get-tuple-element.73), channel_id=1, source_target_pairs={{1,0},{5,1},{2,2},{6,3},{3,4},{7,5},{0,6},{4,7},{9,8},{13,9},{10,1... | collective-permute-start | bytes 1572872 | tf_op jit(solution)/shard_map/ppermute | solution.py:43
  413.1 29.8 %collective-permute-start.21 = (bf16[512,512]{1,0:T(8,128)(2,1)S(1)}, bf16[512,512]{1,0:T(8,128)(2,1)S(1)}, u32[]{:S(2)}, u32[]{:S(2)}) collective-permute-start(bf16[512,512]{1,0:T(8,128)(2,1)S(1)} %get-tuple-element.72), channel_id=1, source_target_pairs={{2,0},{6,1},{3,2},{7,3},{0,4},{4,5},{1,6},{5,7},{10,8},{14,9},{11,... | collective-permute-start | bytes 1572872 | tf_op jit(solution)/shard_map/ppermute | solution.py:43
  413.2 30.6 %collective-permute-start.22 = (bf16[512,512]{1,0:T(8,128)(2,1)S(1)}, bf16[512,512]{1,0:T(8,128)(2,1)S(1)}, u32[]{:S(2)}, u32[]{:S(2)}) collective-permute-start(bf16[512,512]{1,0:T(8,128)(2,1)S(1)} %get-tuple-element.71), channel_id=1, source_target_pairs={{3,0},{7,1},{0,2},{4,3},{1,4},{5,5},{2,6},{6,7},{11,8},{15,9},{8,1... | collective-permute-start | bytes 1572872 | tf_op jit(solution)/shard_map/ppermute | solution.py:43
  459.7 35.2 %collective-permute-start.35 = (bf16[512,512]{1,0:T(8,128)(2,1)S(1)}, bf16[512,512]{1,0:T(8,128)(2,1)S(1)}, u32[]{:S(2)}, u32[]{:S(2)}) collective-permute-start(bf16[512,512]{1,0:T(8,128)(2,1)S(1)} %get-tuple-element.64), channel_id=1, source_target_pairs={{2,0},{6,1},{3,2},{7,3},{0,4},{4,5},{1,6},{5,7},{10,8},{14,9},{11,... | collective-permute-start | bytes 1572872 | tf_op jit(solution)/shard_map/ppermute | solution.py:43
  459.8 35.1 %collective-permute-start.36 = (bf16[512,512]{1,0:T(8,128)(2,1)S(1)}, bf16[512,512]{1,0:T(8,128)(2,1)S(1)}, u32[]{:S(2)}, u32[]{:S(2)}) collective-permute-start(bf16[512,512]{1,0:T(8,128)(2,1)S(1)} %get-tuple-element.63), channel_id=1, source_target_pairs={{3,0},{7,1},{0,2},{4,3},{1,4},{5,5},{2,6},{6,7},{11,8},{15,9},{8,1... | collective-permute-start | bytes 1572872 | tf_op jit(solution)/shard_map/ppermute | solution.py:43
  462.2 32.7 %collective-permute-start.44 = (bf16[512,512]{1,0:T(8,128)(2,1)S(1)}, bf16[512,512]{1,0:T(8,128)(2,1)S(1)}, u32[]{:S(2)}, u32[]{:S(2)}) collective-permute-start(bf16[512,512]{1,0:T(8,128)(2,1)S(1)} %copy-done.6), channel_id=1, source_target_pairs={{0,8},{8,16},{16,24},{24,0},{1,9},{9,17},{17,25},{25,1},{2,10},{10... | collective-permute-start | bytes 1572872 | tf_op jit(solution)/shard_map/ppermute | solution.py:26
  463.6 45.0 %collective-permute-start.45 = (bf16[512,512]{1,0:T(8,128)(2,1)S(1)}, bf16[512,512]{1,0:T(8,128)(2,1)S(1)}, u32[]{:S(2)}, u32[]{:S(2)}) collective-permute-start(bf16[512,512]{1,0:T(8,128)(2,1)S(1)} %copy-done.6), channel_id=1, source_target_pairs={{0,16},{8,24},{16,0},{24,8},{1,17},{9,25},{17,1},{25,9},{2,18},{10... | collective-permute-start | bytes 1572872 | tf_op jit(solution)/shard_map/ppermute | solution.py:26
  475.6 35.2 %collective-permute-start.46 = (bf16[512,512]{1,0:T(8,128)(2,1)S(1)}, bf16[512,512]{1,0:T(8,128)(2,1)S(1)}, u32[]{:S(2)}, u32[]{:S(2)}) collective-permute-start(bf16[512,512]{1,0:T(8,128)(2,1)S(1)} %copy-done.6), channel_id=1, source_target_pairs={{0,24},{8,0},{16,8},{24,16},{1,25},{9,1},{17,9},{25,17},{2,26},{10... | collective-permute-start | bytes 1572872 | tf_op jit(solution)/shard_map/ppermute | solution.py:26
  (56 other events, 888.5 us)
Sparse Core Ops, SparseCore 0:
  226.8 42.8 all-gather.3
  341.1 44.2 all-gather.5
  445.9 54.9 all-gather.7

commit v2 on v1

--- a/solution.py
+++ b/solution.py
@@ -10,9 +10,10 @@
 
 
 def chunk_bounds(width):
-    count = 3 if width % 384 == 0 else 1
-    step = width // count
-    return [(at * step, step) for at in range(count)]
+    unit = width // 6
+    if width % 6 or unit % 128:
+        return [(0, width)]
+    return [(0, unit), (unit, 2 * unit), (3 * unit, 2 * unit), (5 * unit, unit)]
 
 
 def after(value, *earlier):
@@ -78,27 +79,8 @@
     t_keep = jnp.concatenate([rows_of(block_of(col_rank, even, s)) for s in slots[:half]], 0)
     core_pairs = [(c, c ^ 1) for c in range(col_count)]
 
-    def sums(b_part, at_core, at_last):
-        def dot(rows):
-            return jnp.dot(rows, b_part, preferred_element_type=jnp.float32)
-
-        came = lax.ppermute(dot(t_send), "col", core_pairs)
-        came = after(came, *at_core)
-        b_part = after(b_part, came)
-        send = dot(t_pass) + came[half * size :]
-        total = dot(t_keep) + came[: half * size]
-        for level in range(levels):
-            if level > 0:
-                middle = total.shape[0] // 2
-                send, total = total[middle:], total[:middle]
-            pairs = [
-                (c, c ^ (upward[level] if c % 2 == 0 else downward[level]))
-                for c in range(col_count)
-            ]
-            if level == levels - 1:
-                send = after(send, *at_last)
-            total = total + lax.ppermute(send, "col", pairs)
-        return total, came
+    def dot(rows, b_part):
+        return jnp.dot(rows, b_part, preferred_element_type=jnp.float32)
 
     occ_rows = lax.dynamic_slice_in_dim(occ_index, row_rank * row_block, row_block, 0)
     vir_rows = lax.dynamic_slice_in_dim(vir_index, row_rank * row_block, row_block, 0)
@@ -107,39 +89,75 @@
     gap_rows = lookup(occ_rows, occ_energy) - lookup(vir_rows, vir_energy)
     gap_cols = lookup(occ_cols, occ_energy) - lookup(vir_cols, vir_energy)
 
-    chols, b_held = [], []
-    for start, width in chunk_bounds(cholesky.shape[1]):
-        chol = cholesky[:, start : start + width]
-        chols.append(chol)
+    chols = [cholesky[:, at : at + width] for at, width in chunk_bounds(cholesky.shape[1])]
+    count = len(chols)
+    b_held = []
+    for chol in chols:
         first = after(chol, *b_held[-1]) if b_held else chol
         b_held.append(along_rows(first, row_count))
 
-    came, x_held, x_rows, x_cols = None, [], [], []
+    x_held, x_rows, x_cols = [], [], []
+    b_cols = to_columns(b_held[0], row_count, col_count)
+    if count > 1:
+        b_cols = after(b_cols, b_held[1][1])
+    sent = dot(t_send, b_cols)
     for at, chol in enumerate(chols):
-        held = b_held[at]
-        if at > 0:
+        beside = x_held[-1] if at > 0 else []
+        came = lax.ppermute(sent, "col", core_pairs)
+        b_next = None
+        if at + 1 < count:
+            held = b_held[at + 1]
             held = lax.optimization_barrier((*held, came))[: len(held)]
-        b_cols = to_columns(held, row_count, col_count)
-        if at > 0:
-            b_cols = after(b_cols, x_held[-1][0])
-        elif len(chols) > 1:
-            b_cols = after(b_cols, *b_held[1])
-        beside = x_held[-1] if at > 0 else b_held[min(2, len(chols) - 1)]
-        at_last = beside[2:] + (x_rows[-1:] if at > 0 else [])
-        summed, came = sums(b_cols, beside[1:2], at_last)
-        x_piece = (chol.astype(jnp.float32) + summed).astype(jnp.bfloat16)
+            b_next = to_columns(held, row_count, col_count)
+        b_cols = after(b_cols, came)
+        send = dot(t_pass, b_cols) + came[half * size :]
+        total = dot(t_keep, b_cols) + came[: half * size]
+        for level in range(levels):
+            if level > 0:
+                middle = total.shape[0] // 2
+                send, total = total[middle:], total[:middle]
+            if level == levels - 1:
+                send = after(send, *beside[1:2])
+                if at > 0:
+                    send = after(send, x_rows[at - 1])
+                if at + 2 < count:
+                    send = after(send, b_held[at + 2][1])
+                if b_next is not None:
+                    send = after(send, b_next)
+            pairs = [
+                (c, c ^ (upward[level] if c % 2 == 0 else downward[level]))
+                for c in range(col_count)
+            ]
+            total = total + lax.ppermute(send, "col", pairs)
+        x_piece = (chol.astype(jnp.float32) + total).astype(jnp.bfloat16)
+        x_piece = after(x_piece, *beside[2:])
         if at > 1:
             x_piece = after(x_piece, x_cols[at - 2])
+        if b_next is not None:
+            b_cols = b_next
+            sent = dot(t_send, b_cols)
+            x_piece = after(x_piece, sent)
         x_rows.append(lax.all_gather(x_piece, "col", axis=0, tiled=True))
         x_held.append(along_rows(x_piece, row_count))
-        x_cols.append(to_columns(x_held[-1], row_count, col_count))
+        if at + 1 < count or count < 3:
+            x_cols.append(to_columns(x_held[-1], row_count, col_count))
 
-    product = None
-    for rows, cols in zip(x_rows, x_cols):
-        term = lax.dot_general(
-            rows, cols, (((1,), (1,)), ((), ())), preferred_element_type=jnp.float32
+    def product_of(first, last):
+        return lax.dot_general(
+            jnp.concatenate(x_rows[first:last], 1),
+            jnp.concatenate(x_cols[first:last], 1),
+            (((1,), (1,)), ((), ())),
+            preferred_element_type=jnp.float32,
         )
-        product = term if product is None else product + term
+
+    if count < 3:
+        product = product_of(0, count)
+    else:
+        product = product_of(0, count - 2)
+        held = lax.optimization_barrier((*x_held[-1], product))
+        x_cols.append(to_columns(held[:-1], row_count, col_count))
+        product = held[-1] + product_of(count - 2, count - 1)
+        product = product + product_of(count - 1, count)
     return accumulated + product / (gap_rows[:, None] + gap_cols[None, :])
 
 

time: 605 us -> 654 us (1.081)
  starting transfers between devices: 84.3 us -> 127 us
  local copies, waits for them, and re-layouts: 47.6 us -> 38.2 us
  other arithmetic: 21.3 us -> 30.1 us
  matrix products: 132 us -> 139 us
    ppermute x9 -> x12, waiting for transfers between devices: 80.5 us -> 31 us  [the longest x8 24.8 us: on_device(): total = total + lax.ppermute(send, 'col', pairs)]
    ppermute x18 -> x24, waiting for transfers between devices: 124 us -> 173 us  [along_rows(): held.append(lax.ppermute(piece, 'row', pairs))]
    ppermute x24 -> x32, starting transfers between devices: 57.6 us -> 94.8 us  [to_columns(): got = lax.ppermute(send, 'col', pairs)]
    ppermute x18 -> x24, starting transfers between devices: 15.5 us -> 29.7 us  [along_rows(): held.append(lax.ppermute(piece, 'row', pairs))]
    ppermute x9 -> x12, starting transfers between devices: 11.2 us -> 2.4 us  [the longest x4 1.32 us: on_device(): came = lax.ppermute(sent, 'col', core_pairs)]
    dot_general x9 -> x12, matrix products: 52.1 us -> 57.4 us  [dot(): return jnp.dot(rows, b_part, preferred_element_type=jnp.float32)]
    dynamic_update_slice x24 -> x32, local copies, waits for them, and re-layouts: 18.6 us -> 16.9 us  [to_columns(): out = lax.dynamic_update_slice_in_dim(out, got, place * size, 0)]
    ppermute x24 -> x32, waiting for transfers between devices: 91.1 us -> 89.4 us  [to_columns(): got = lax.ppermute(send, 'col', pairs)]
  transfers between devices with their start and end apart: 54 -> 72, of which waited for: 26 -> 34; matrix products, arithmetic and copies ran while one was open for 18% -> 22% of each run, Pallas kernels for 0% -> 0%
where the time goes in v2:
time: 654 us; the launch traced here: 643 us
  waiting for transfers between devices  293 us (45%)
  matrix products  139 us (21%)
  starting transfers between devices  127 us (19%)
  local copies, waits for them, and re-layouts  38.2 us (6%)
  other arithmetic  30.1 us (5%)
  between operations  14.8 us (2%)
    ppermute x24, waiting for transfers between devices, along_rows(): held.append(lax.ppermute(piece, 'row', pairs))  173 us
    ppermute x32, starting transfers between devices, to_columns(): got = lax.ppermute(send, 'col', pairs)  94.8 us
    ppermute x32, waiting for transfers between devices, to_columns(): got = lax.ppermute(send, 'col', pairs)  89.4 us
    dot_general x3, matrix products, product_of(): lax.dot_general(jnp.concatenate(x_rows[first:last], 1), jnp.concatenate(x...  81.9 us
    dot_general x12, matrix products, dot(): return jnp.dot(rows, b_part, preferred_element_type=jnp.float32)  57.4 us
    ppermute x24, starting transfers between devices, along_rows(): held.append(lax.ppermute(piece, 'row', pairs))  29.7 us
    ppermute x8, waiting for transfers between devices, on_device(): total = total + lax.ppermute(send, 'col', pairs)  24.8 us
    dynamic_update_slice x32, local copies, waits for them, and re-layouts, to_columns(): out = lax.dynamic_update_slice_in_dim(out, got, place * size, 0)  16.9 us
  transfers between devices with their start and end apart: 72, of which 34 were waited for; matrix products, arithmetic and copies ran while one was open for 22% of the time, Pallas kernels for 0%

profile of v2, /device:TPU:11, one launch (start us, length us, event | category | flops | bytes accessed | tf_op | source)
XLA Modules:
  0.0 642.8 jit_solution(55868053617006215)
XLA Ops:
  12.2 10.1 %constant_dynamic-slice_fusion.7 = (bf16[512,2048]{1,0:T(8,128)(2,1)}, bf16[512,2048]{1,0:T(8,128)(2,1)S(1)}, bf16[512,2048]{1,0:T(8,128)(2,1)S(1)}, bf16[512,20...) fusion(bf16[4096,2048]{1,0:T(8,128)(2,1)} %param.7, ...), kind=kLoop, calls=%fused_computation.114 | loop fusion | bytes 33554464 | tf_op jit(solution)/shard_map/dynamic_slice | solution.py:72
  22.4 9.4 %collective-permute-done.1 = bf16[512,256]{1,0:T(8,128)(2,1)S(1)} collective-permute-done((bf16[512,256]{1,0:T(8,128)(2,1)}, bf16[512,256]{1,0:T(8,128)(2,1)S(1)}, u32[]{:S(2)}, u32[]{:S(2)}) %collective-permute-start.1) | collective-permute-done | bytes 262176 | tf_op jit(solution)/shard_map/ppermute | solution.py:27
  57.5 5.9 fusion.24
  67.3 31.6 %collective-permute-done.4 = bf16[512,512]{1,0:T(8,128)(2,1)S(1)} collective-permute-done((bf16[512,512]{1,0:T(8,128)(2,1)S(1)}, bf16[512,512]{1,0:T(8,128)(2,1)S(1)}, u32[]{:S(2)}, u32[]{:S(2)}) %collective-permute-start.4) | collective-permute-done | bytes 524320 | tf_op jit(solution)/shard_map/ppermute | solution.py:27
  109.4 6.3 collective-permute-done.17
  115.9 10.4 %collective-permute-done.18 = bf16[512,512]{1,0:T(8,128)(2,1)S(1)} collective-permute-done((bf16[512,512]{1,0:T(8,128)(2,1)S(1)}, bf16[512,512]{1,0:T(8,128)(2,1)S(1)}, u32[]{:S(2)}, u32[]{:S(2)}) %collective-permute-start.18) | collective-permute-done | bytes 524320 | tf_op jit(solution)/shard_map/ppermute | solution.py:44
  128.9 6.0 fusion.25
  136.6 13.9 %collective-permute-done.35 = f32[1024,256]{1,0:T(8,128)S(1)} collective-permute-done((f32[1024,256]{1,0:T(8,128)S(1)}, f32[1024,256]{1,0:T(8,128)S(1)}, u32[]{:S(2)}, u32[]{:S(2)}) %collective-permute-start.35) | collective-permute-done | bytes 1048608 | tf_op jit(solution)/shard_map/ppermute | solution.py:131
  152.4 7.8 %collective-permute-done.36 = f32[512,256]{1,0:T(8,128)S(1)} collective-permute-done((f32[512,256]{1,0:T(8,128)S(1)}, f32[512,256]{1,0:T(8,128)S(1)}, u32[]{:S(2)}, u32[]{:S(2)}) %collective-permute-start.36) | collective-permute-done | bytes 524320 | tf_op jit(solution)/shard_map/ppermute | solution.py:131
  161.3 5.9 slice_add_fusion
  169.3 32.9 %collective-permute-done.7 = bf16[512,512]{1,0:T(8,128)(2,1)S(1)} collective-permute-done((bf16[512,512]{1,0:T(8,128)(2,1)S(1)}, bf16[512,512]{1,0:T(8,128)(2,1)S(1)}, u32[]{:S(2)}, u32[]{:S(2)}) %collective-permute-start.7) | collective-permute-done | bytes 524320 | tf_op jit(solution)/shard_map/ppermute | solution.py:27
  219.5 11.3 %collective-permute-done.23 = bf16[512,512]{1,0:T(8,128)(2,1)S(1)} collective-permute-done((bf16[512,512]{1,0:T(8,128)(2,1)S(1)}, bf16[512,512]{1,0:T(8,128)(2,1)S(1)}, u32[]{:S(2)}, u32[]{:S(2)}) %collective-permute-start.23) | collective-permute-done | bytes 524320 | tf_op jit(solution)/shard_map/ppermute | solution.py:44
  237.8 9.0 %collective-permute-done.37 = bf16[512,256]{1,0:T(8,128)(2,1)} collective-permute-done((bf16[512,256]{1,0:T(8,128)(2,1)S(1)}, bf16[512,256]{1,0:T(8,128)(2,1)}, u32[]{:S(2)}, u32[]{:S(2)}) %collective-permute-start.37) | collective-permute-done | bytes 262176 | tf_op jit(solution)/shard_map/ppermute | solution.py:27
  246.8 10.6 %fusion.26 = f32[2048,512]{1,0:T(8,128)} fusion(bf16[2048,2048]{1,0:T(8,128)(2,1)} %pad_maximum_fusion, bf16[2048,512]{1,0:T(8,128)(2,1)} %copy-done.17), kind=kOutput, calls=%fused_computation.122 | convolution fusion | flops 4294967296 | bytes 14680064 | tf_op jit(solution)/shard_map/dot_general | solution.py:83
  264.8 5.9 slice_add_fusion.2
  284.3 29.2 %collective-permute-done.45 = bf16[512,256]{1,0:T(8,128)(2,1)S(1)} collective-permute-done((bf16[512,256]{1,0:T(8,128)(2,1)S(1)}, bf16[512,256]{1,0:T(8,128)(2,1)S(1)}, u32[]{:S(2)}, u32[]{:S(2)}) %collective-permute-start.45) | collective-permute-done | bytes 262176 | tf_op jit(solution)/shard_map/ppermute | solution.py:44
  315.2 7.2 %collective-permute-start.27 = (bf16[512,256]{1,0:T(8,128)(2,1)S(1)}, bf16[512,256]{1,0:T(8,128)(2,1)S(1)}, u32[]{:S(2)}, u32[]{:S(2)}) collective-permute-start(bf16[512,256]{1,0:T(8,128)(2,1)S(1)} %get-tuple-element.136), channel_id=1, source_target_pairs={{0,0},{4,1},{1,2},{5,3},{2,4},{6,5},{3,6},{7,7},{8,8},{12,9},{9,10... | collective-permute-start | bytes 786440 | tf_op jit(solution)/shard_map/ppermute | solution.py:44
  345.8 6.4 collective-permute-done.41
  359.7 7.3 %fusion.27 = f32[2048,256]{1,0:T(8,128)} fusion(bf16[2048,2048]{1,0:T(8,128)(2,1)} %pad_maximum_fusion, bf16[2048,256]{1,0:T(8,128)(2,1)} %copy-done.24), kind=kOutput, calls=%fused_computation.123 | convolution fusion | flops 2147483648 | bytes 11534336 | tf_op jit(solution)/shard_map/dot_general | solution.py:83
  369.1 22.6 %collective-permute-done.43 = bf16[512,512]{1,0:T(8,128)(2,1)} collective-permute-done((bf16[512,512]{1,0:T(8,128)(2,1)S(1)}, bf16[512,512]{1,0:T(8,128)(2,1)}, u32[]{:S(2)}, u32[]{:S(2)}) %collective-permute-start.43) | collective-permute-done | bytes 524320 | tf_op jit(solution)/shard_map/ppermute | solution.py:27
  416.3 6.2 collective-permute-start.56
  422.6 11.0 %collective-permute-done.53 = bf16[512,512]{1,0:T(8,128)(2,1)} collective-permute-done((bf16[512,512]{1,0:T(8,128)(2,1)}, bf16[512,512]{1,0:T(8,128)(2,1)}, u32[]{:S(2)}, u32[]{:S(2)}) %collective-permute-start.53) | collective-permute-done | bytes 524320 | tf_op jit(solution)/shard_map/ppermute | solution.py:44
  434.8 7.6 %collective-permute-start.49 = (bf16[512,512]{1,0:T(8,128)(2,1)S(1)}, bf16[512,512]{1,0:T(8,128)(2,1)}, u32[]{:S(2)}, u32[]{:S(2)}) collective-permute-start(bf16[512,512]{1,0:T(8,128)(2,1)S(1)} %copy-done.2), channel_id=1, source_target_pairs={{0,8},{8,16},{16,24},{24,0},{1,9},{9,17},{17,25},{25,1},{2,10},{10... | collective-permute-start | bytes 1572872 | tf_op jit(solution)/shard_map/ppermute | solution.py:27
  448.5 25.6 %collective-permute-done.49 = bf16[512,512]{1,0:T(8,128)(2,1)} collective-permute-done((bf16[512,512]{1,0:T(8,128)(2,1)S(1)}, bf16[512,512]{1,0:T(8,128)(2,1)}, u32[]{:S(2)}, u32[]{:S(2)}) %collective-permute-start.49) | collective-permute-done | bytes 524320 | tf_op jit(solution)/shard_map/ppermute | solution.py:27
  477.8 7.5 %collective-permute-done.51 = bf16[512,512]{1,0:T(8,128)(2,1)S(1)} collective-permute-done((bf16[512,512]{1,0:T(8,128)(2,1)S(1)}, bf16[512,512]{1,0:T(8,128)(2,1)S(1)}, u32[]{:S(2)}, u32[]{:S(2)}) %collective-permute-start.51) | collective-permute-done | bytes 524320 | tf_op jit(solution)/shard_map/ppermute | solution.py:27
  488.8 7.2 %collective-permute-start.60 = (bf16[512,512]{1,0:T(8,128)(2,1)}, bf16[512,512]{1,0:T(8,128)(2,1)}, u32[]{:S(2)}, u32[]{:S(2)}) collective-permute-start(bf16[512,512]{1,0:T(8,128)(2,1)} %get-tuple-element.108), channel_id=1, source_target_pairs={{0,0},{4,1},{1,2},{5,3},{2,4},{6,5},{3,6},{7,7},{8,8},{12,9},{9,10... | collective-permute-start | bytes 1572872 | tf_op jit(solution)/shard_map/ppermute | solution.py:44
  496.0 8.6 %collective-permute-start.61 = (bf16[512,512]{1,0:T(8,128)(2,1)}, bf16[512,512]{1,0:T(8,128)(2,1)}, u32[]{:S(2)}, u32[]{:S(2)}) collective-permute-start(bf16[512,512]{1,0:T(8,128)(2,1)} %get-tuple-element.107), channel_id=1, source_target_pairs={{1,0},{5,1},{2,2},{6,3},{3,4},{7,5},{0,6},{4,7},{9,8},{13,9},{10,1... | collective-permute-start | bytes 1572872 | tf_op jit(solution)/shard_map/ppermute | solution.py:44
  512.4 22.7 %fusion = f32[4096,2048]{1,0:T(8,128)} fusion(bf16[4096,512]{1,0:T(8,128)(2,1)} %all-gather.7.cloned.1.call-done, bf16[4096,256]{1,0:T(8,128)(2,1)} %all-gather.5.cloned.1.call-done, bf16[2048,512]{1,0:T(8,128)(2,1)S(1)} %copy-done.20, bf16[2048,256]{1,0:T(8,128)(2,1)} %constant_dynamic-update-slice_fusion.12), kind=kOutput, calls=%fused_computation.2 | convolution fusion | flops 12903776256 | bytes 42991616 | tf_op jit(solution)/shard_map/dot_general | solution.py:146
  544.4 14.9 %collective-permute-done.58 = bf16[512,256]{1,0:T(8,128)(2,1)S(1)} collective-permute-done((bf16[512,256]{1,0:T(8,128)(2,1)S(1)}, bf16[512,256]{1,0:T(8,128)(2,1)S(1)}, u32[]{:S(2)}, u32[]{:S(2)}) %collective-permute-start.58) | collective-permute-done | bytes 262176 | tf_op jit(solution)/shard_map/ppermute | solution.py:27
  567.4 14.4 %fusion.28 = f32[4096,2048]{1,0:T(8,128)} fusion(bf16[4096,512]{1,0:T(8,128)(2,1)S(1)} %copy-done.34, bf16[2048,512]{1,0:T(8,128)(2,1)S(1)} %constant_dynamic-update-slice_fusion.4), kind=kOutput, calls=%fused_computation.124 | convolution fusion | flops 8589934592 | bytes 39845888 | tf_op jit(solution)/shard_map/dot_general | solution.py:146
  583.9 7.1 %collective-permute-done.67 = bf16[512,256]{1,0:T(8,128)(2,1)S(1)} collective-permute-done((bf16[512,256]{1,0:T(8,128)(2,1)S(1)}, bf16[512,256]{1,0:T(8,128)(2,1)S(1)}, u32[]{:S(2)}, u32[]{:S(2)}) %collective-permute-start.67) | collective-permute-done | bytes 262176 | tf_op jit(solution)/shard_map/ppermute | solution.py:44
  591.1 44.8 %divide_add_fusion = f32[4096,2048]{1,0:T(8,128)} fusion(f32[4096,2048]{1,0:T(8,128)} %param.8, f32[4096,2048]{1,0:T(8,128)} %fusion, f32[4096,2048]{1,0:T(8,128)} %fusion.28, f32[2048]{0:T(1024)S(1)} %sub.128, f32[4096]{0:T(1024)S(1)} %sub.127, bf16[4096,256]{1,0:T(8,128)(2,1)} %all-gather.11.cloned.1.call-done, ...), kind=kOutput, calls=%fused_computation | convolution fusion | flops 4336910336 | bytes 137388032 | tf_op jit(solution)/shard_map/dot_general | solution.py:146
  (282 shorter events, 200.7 us)
Async XLA Ops:
  6.5 240.2 %all-gather.5.cloned.1.call-start = ((), (), s32[]{:S(2)}) async-start(), calls=%async_computation | async-start | bytes 2359296 | tf_op jit(solution)/shard_map/all_gather | solution.py:140
  63.4 37.4 %collective-permute-start.16 = (f32[2048,256]{1,0:T(8,128)S(1)}, f32[2048,256]{1,0:T(8,128)S(1)}, u32[]{:S(2)}, u32[]{:S(2)}) collective-permute-start(f32[2048,256]{1,0:T(8,128)S(1)} %fusion.24), channel_id=1, source_target_pairs={{0,1},{1,0},{2,3},{3,2},{4,5},{5,4},{6,7},{7,6},{8,9},{9,8},{10,11... | collective-permute-start | bytes 6291464 | tf_op jit(solution)/shard_map/ppermute | solution.py:106
  63.5 35.4 %collective-permute-start.4 = (bf16[512,512]{1,0:T(8,128)(2,1)S(1)}, bf16[512,512]{1,0:T(8,128)(2,1)S(1)}, u32[]{:S(2)}, u32[]{:S(2)}) collective-permute-start(bf16[512,512]{1,0:T(8,128)(2,1)S(1)} %get-tuple-element.53), channel_id=1, source_target_pairs={{0,16},{8,24},{16,0},{24,8},{1,17},{9,25},{17,1},{25,9},{2,18},{10... | collective-permute-start | bytes 1572872 | tf_op jit(solution)/shard_map/ppermute | solution.py:27
  65.6 35.3 %collective-permute-start.5 = (bf16[512,512]{1,0:T(8,128)(2,1)S(1)}, bf16[512,512]{1,0:T(8,128)(2,1)S(1)}, u32[]{:S(2)}, u32[]{:S(2)}) collective-permute-start(bf16[512,512]{1,0:T(8,128)(2,1)S(1)} %get-tuple-element.53), channel_id=1, source_target_pairs={{0,24},{8,0},{16,8},{24,16},{1,25},{9,1},{17,9},{25,17},{2,26},{10... | collective-permute-start | bytes 1572872 | tf_op jit(solution)/shard_map/ppermute | solution.py:27
  161.0 191.2 %all-gather.7.cloned.1.call-start = ((), (), s32[]{:S(2)}) async-start(), calls=%async_computation.1 | async-start | bytes 4718592 | tf_op jit(solution)/shard_map/all_gather | solution.py:140
  167.2 68.1 %collective-permute-start.34 = (f32[1024,512]{1,0:T(8,128)S(1)}, f32[1024,512]{1,0:T(8,128)S(1)}, u32[]{:S(2)}, u32[]{:S(2)}) collective-permute-start(f32[1024,512]{1,0:T(8,128)S(1)} %slice_add_fusion), channel_id=1, source_target_pairs={{0,2},{1,5},{2,0},{3,7},{4,6},{5,1},{6,4},{7,3},{8,10},{9,13},{10,... | collective-permute-start | bytes 6291464 | tf_op jit(solution)/shard_map/ppermute | solution.py:131
  167.5 34.8 %collective-permute-start.7 = (bf16[512,512]{1,0:T(8,128)(2,1)S(1)}, bf16[512,512]{1,0:T(8,128)(2,1)S(1)}, u32[]{:S(2)}, u32[]{:S(2)}) collective-permute-start(bf16[512,512]{1,0:T(8,128)(2,1)S(1)} %get-tuple-element.57), channel_id=1, source_target_pairs={{0,16},{8,24},{16,0},{24,8},{1,17},{9,25},{17,1},{25,9},{2,18},{10... | collective-permute-start | bytes 1572872 | tf_op jit(solution)/shard_map/ppermute | solution.py:27
  169.3 34.9 %collective-permute-start.8 = (bf16[512,512]{1,0:T(8,128)(2,1)S(1)}, bf16[512,512]{1,0:T(8,128)(2,1)S(1)}, u32[]{:S(2)}, u32[]{:S(2)}) collective-permute-start(bf16[512,512]{1,0:T(8,128)(2,1)S(1)} %get-tuple-element.57), channel_id=1, source_target_pairs={{0,24},{8,0},{16,8},{24,16},{1,25},{9,1},{17,9},{25,17},{2,26},{10... | collective-permute-start | bytes 1572872 | tf_op jit(solution)/shard_map/ppermute | solution.py:27
  219.3 27.5 %collective-permute-start.9 = (bf16[512,256]{1,0:T(8,128)(2,1)}, bf16[512,256]{1,0:T(8,128)(2,1)}, u32[]{:S(2)}, u32[]{:S(2)}) collective-permute-start(bf16[512,256]{1,0:T(8,128)(2,1)} %get-tuple-element.61), channel_id=1, source_target_pairs={{0,8},{8,16},{16,24},{24,0},{1,9},{9,17},{17,25},{25,1},{2,10},{10... | collective-permute-start | bytes 786440 | tf_op jit(solution)/shard_map/ppermute | solution.py:27
  232.7 29.9 %collective-permute-start.39 = (bf16[512,256]{1,0:T(8,128)(2,1)S(1)}, bf16[512,256]{1,0:T(8,128)(2,1)}, u32[]{:S(2)}, u32[]{:S(2)}) collective-permute-start(bf16[512,256]{1,0:T(8,128)(2,1)S(1)} %copy-done.3), channel_id=1, source_target_pairs={{0,16},{8,24},{16,0},{24,8},{1,17},{9,25},{17,1},{25,9},{2,18},{10... | collective-permute-start | bytes 786440 | tf_op jit(solution)/shard_map/ppermute | solution.py:27
  233.8 28.8 %collective-permute-start.40 = (bf16[512,256]{1,0:T(8,128)(2,1)S(1)}, bf16[512,256]{1,0:T(8,128)(2,1)}, u32[]{:S(2)}, u32[]{:S(2)}) collective-permute-start(bf16[512,256]{1,0:T(8,128)(2,1)S(1)} %copy-done.3), channel_id=1, source_target_pairs={{0,24},{8,0},{16,8},{24,16},{1,25},{9,1},{17,9},{25,17},{2,26},{10... | collective-permute-start | bytes 786440 | tf_op jit(solution)/shard_map/ppermute | solution.py:27
  262.6 211.5 %all-gather.9.cloned.1.call-start = ((), (), s32[]{:S(2)}) async-start(), calls=%async_computation.2 | async-start | bytes 4718592 | tf_op jit(solution)/shard_map/all_gather | solution.py:140
  270.8 71.6 %collective-permute-start.33 = (f32[1024,512]{1,0:T(8,128)S(1)}, f32[1024,512]{1,0:T(8,128)S(1)}, u32[]{:S(2)}, u32[]{:S(2)}) collective-permute-start(f32[1024,512]{1,0:T(8,128)S(1)} %slice_add_fusion.2), channel_id=1, source_target_pairs={{0,2},{1,5},{2,0},{3,7},{4,6},{5,1},{6,4},{7,3},{8,10},{9,13},{10,... | collective-permute-start | bytes 6291464 | tf_op jit(solution)/shard_map/ppermute | solution.py:131
  273.1 40.4 %collective-permute-start.45 = (bf16[512,256]{1,0:T(8,128)(2,1)S(1)}, bf16[512,256]{1,0:T(8,128)(2,1)S(1)}, u32[]{:S(2)}, u32[]{:S(2)}) collective-permute-start(bf16[512,256]{1,0:T(8,128)(2,1)S(1)} %get-tuple-element.132), channel_id=1, source_target_pairs={{0,0},{4,1},{1,2},{5,3},{2,4},{6,5},{3,6},{7,7},{8,8},{12,9},{9,10... | collective-permute-start | bytes 786440 | tf_op jit(solution)/shard_map/ppermute | solution.py:44
  275.2 38.4 %collective-permute-start.10 = (bf16[512,256]{1,0:T(8,128)(2,1)}, bf16[512,256]{1,0:T(8,128)(2,1)S(1)}, u32[]{:S(2)}, u32[]{:S(2)}) collective-permute-start(bf16[512,256]{1,0:T(8,128)(2,1)} %get-tuple-element.61), channel_id=1, source_target_pairs={{0,16},{8,24},{16,0},{24,8},{1,17},{9,25},{17,1},{25,9},{2,18},{10... | collective-permute-start | bytes 786440 | tf_op jit(solution)/shard_map/ppermute | solution.py:27
  275.3 38.4 %collective-permute-start.11 = (bf16[512,256]{1,0:T(8,128)(2,1)}, bf16[512,256]{1,0:T(8,128)(2,1)S(1)}, u32[]{:S(2)}, u32[]{:S(2)}) collective-permute-start(bf16[512,256]{1,0:T(8,128)(2,1)} %get-tuple-element.61), channel_id=1, source_target_pairs={{0,24},{8,0},{16,8},{24,16},{1,25},{9,1},{17,9},{25,17},{2,26},{10... | collective-permute-start | bytes 786440 | tf_op jit(solution)/shard_map/ppermute | solution.py:27
  278.5 73.7 %collective-permute-start.46 = (bf16[512,256]{1,0:T(8,128)(2,1)}, bf16[512,256]{1,0:T(8,128)(2,1)}, u32[]{:S(2)}, u32[]{:S(2)}) collective-permute-start(bf16[512,256]{1,0:T(8,128)(2,1)} %get-tuple-element.131), channel_id=1, source_target_pairs={{1,0},{5,1},{2,2},{6,3},{3,4},{7,5},{0,6},{4,7},{9,8},{13,9},{10,1... | collective-permute-start | bytes 786440 | tf_op jit(solution)/shard_map/ppermute | solution.py:44
  357.3 34.4 %collective-permute-start.43 = (bf16[512,512]{1,0:T(8,128)(2,1)S(1)}, bf16[512,512]{1,0:T(8,128)(2,1)}, u32[]{:S(2)}, u32[]{:S(2)}) collective-permute-start(bf16[512,512]{1,0:T(8,128)(2,1)S(1)} %copy-done.1), channel_id=1, source_target_pairs={{0,16},{8,24},{16,0},{24,8},{1,17},{9,25},{17,1},{25,9},{2,18},{10... | collective-permute-start | bytes 1572872 | tf_op jit(solution)/shard_map/ppermute | solution.py:27
  358.0 35.0 %collective-permute-start.44 = (bf16[512,512]{1,0:T(8,128)(2,1)S(1)}, bf16[512,512]{1,0:T(8,128)(2,1)}, u32[]{:S(2)}, u32[]{:S(2)}) collective-permute-start(bf16[512,512]{1,0:T(8,128)(2,1)S(1)} %copy-done.1), channel_id=1, source_target_pairs={{0,24},{8,0},{16,8},{24,16},{1,25},{9,1},{17,9},{25,17},{2,26},{10... | collective-permute-start | bytes 1572872 | tf_op jit(solution)/shard_map/ppermute | solution.py:27
  393.0 198.1 %all-gather.11.cloned.1.call-start = ((), (), s32[]{:S(2)}) async-start(), calls=%async_computation.3 | async-start | bytes 2359296 | tf_op jit(solution)/shard_map/all_gather | solution.py:140
  404.0 39.7 %collective-permute-start.32 = (f32[1024,256]{1,0:T(8,128)}, f32[1024,256]{1,0:T(8,128)}, u32[]{:S(2)}, u32[]{:S(2)}) collective-permute-start(f32[1024,256]{1,0:T(8,128)} %convolution_add_fusion.2), channel_id=1, source_target_pairs={{0,2},{1,5},{2,0},{3,7},{4,6},{5,1},{6,4},{7,3},{8,10},{9,13},{10,... | collective-permute-start | bytes 3145736 | tf_op jit(solution)/shard_map/ppermute | solution.py:131
  411.6 30.8 %collective-permute-start.54 = (bf16[512,512]{1,0:T(8,128)(2,1)}, bf16[512,512]{1,0:T(8,128)(2,1)S(1)}, u32[]{:S(2)}, u32[]{:S(2)}) collective-permute-start(bf16[512,512]{1,0:T(8,128)(2,1)} %get-tuple-element.111), channel_id=1, source_target_pairs={{1,0},{5,1},{2,2},{6,3},{3,4},{7,5},{0,6},{4,7},{9,8},{13,9},{10,1... | collective-permute-start | bytes 1572872 | tf_op jit(solution)/shard_map/ppermute | solution.py:44
  416.3 57.8 %collective-permute-start.55 = (bf16[512,512]{1,0:T(8,128)(2,1)}, bf16[512,512]{1,0:T(8,128)(2,1)}, u32[]{:S(2)}, u32[]{:S(2)}) collective-permute-start(bf16[512,512]{1,0:T(8,128)(2,1)} %get-tuple-element.110), channel_id=1, source_target_pairs={{2,0},{6,1},{3,2},{7,3},{0,4},{4,5},{1,6},{5,7},{10,8},{14,9},{11,... | collective-permute-start | bytes 1572872 | tf_op jit(solution)/shard_map/ppermute | solution.py:44
  416.3 59.6 %collective-permute-start.56 = (bf16[512,512]{1,0:T(8,128)(2,1)}, bf16[512,512]{1,0:T(8,128)(2,1)}, u32[]{:S(2)}, u32[]{:S(2)}) collective-permute-start(bf16[512,512]{1,0:T(8,128)(2,1)} %get-tuple-element.109), channel_id=1, source_target_pairs={{3,0},{7,1},{0,2},{4,3},{1,4},{5,5},{2,6},{6,7},{11,8},{15,9},{8,1... | collective-permute-start | bytes 1572872 | tf_op jit(solution)/shard_map/ppermute | solution.py:44
  434.8 39.3 %collective-permute-start.49 = (bf16[512,512]{1,0:T(8,128)(2,1)S(1)}, bf16[512,512]{1,0:T(8,128)(2,1)}, u32[]{:S(2)}, u32[]{:S(2)}) collective-permute-start(bf16[512,512]{1,0:T(8,128)(2,1)S(1)} %copy-done.2), channel_id=1, source_target_pairs={{0,8},{8,16},{16,24},{24,0},{1,9},{9,17},{17,25},{25,1},{2,10},{10... | collective-permute-start | bytes 1572872 | tf_op jit(solution)/shard_map/ppermute | solution.py:27
  442.5 42.9 %collective-permute-start.51 = (bf16[512,512]{1,0:T(8,128)(2,1)S(1)}, bf16[512,512]{1,0:T(8,128)(2,1)S(1)}, u32[]{:S(2)}, u32[]{:S(2)}) collective-permute-start(bf16[512,512]{1,0:T(8,128)(2,1)S(1)} %copy-done.2), channel_id=1, source_target_pairs={{0,16},{8,24},{16,0},{24,8},{1,17},{9,25},{17,1},{25,9},{2,18},{10... | collective-permute-start | bytes 1572872 | tf_op jit(solution)/shard_map/ppermute | solution.py:27
  443.8 42.4 %collective-permute-start.52 = (bf16[512,512]{1,0:T(8,128)(2,1)S(1)}, bf16[512,512]{1,0:T(8,128)(2,1)}, u32[]{:S(2)}, u32[]{:S(2)}) collective-permute-start(bf16[512,512]{1,0:T(8,128)(2,1)S(1)} %copy-done.2), channel_id=1, source_target_pairs={{0,24},{8,0},{16,8},{24,16},{1,25},{9,1},{17,9},{25,17},{2,26},{10... | collective-permute-start | bytes 1572872 | tf_op jit(solution)/shard_map/ppermute | solution.py:27
  474.1 36.5 %collective-permute-start.50 = (f32[512,256]{1,0:T(8,128)}, f32[512,256]{1,0:T(8,128)S(1)}, u32[]{:S(2)}, u32[]{:S(2)}) collective-permute-start(f32[512,256]{1,0:T(8,128)} %slice.83), channel_id=1, source_target_pairs={{0,4},{1,3},{2,6},{3,1},{4,0},{5,7},{6,2},{7,5},{8,12},{9,11},{10,... | collective-permute-start | bytes 1572872 | tf_op jit(solution)/shard_map/ppermute | solution.py:131
  488.8 46.4 %collective-permute-start.60 = (bf16[512,512]{1,0:T(8,128)(2,1)}, bf16[512,512]{1,0:T(8,128)(2,1)}, u32[]{:S(2)}, u32[]{:S(2)}) collective-permute-start(bf16[512,512]{1,0:T(8,128)(2,1)} %get-tuple-element.108), channel_id=1, source_target_pairs={{0,0},{4,1},{1,2},{5,3},{2,4},{6,5},{3,6},{7,7},{8,8},{12,9},{9,10... | collective-permute-start | bytes 1572872 | tf_op jit(solution)/shard_map/ppermute | solution.py:44
  496.0 43.7 %collective-permute-start.61 = (bf16[512,512]{1,0:T(8,128)(2,1)}, bf16[512,512]{1,0:T(8,128)(2,1)}, u32[]{:S(2)}, u32[]{:S(2)}) collective-permute-start(bf16[512,512]{1,0:T(8,128)(2,1)} %get-tuple-element.107), channel_id=1, source_target_pairs={{1,0},{5,1},{2,2},{6,3},{3,4},{7,5},{0,6},{4,7},{9,8},{13,9},{10,1... | collective-permute-start | bytes 1572872 | tf_op jit(solution)/shard_map/ppermute | solution.py:44
  504.6 37.6 %collective-permute-start.62 = (bf16[512,512]{1,0:T(8,128)(2,1)}, bf16[512,512]{1,0:T(8,128)(2,1)}, u32[]{:S(2)}, u32[]{:S(2)}) collective-permute-start(bf16[512,512]{1,0:T(8,128)(2,1)} %get-tuple-element.106), channel_id=1, source_target_pairs={{2,0},{6,1},{3,2},{7,3},{0,4},{4,5},{1,6},{5,7},{10,8},{14,9},{11,... | collective-permute-start | bytes 1572872 | tf_op jit(solution)/shard_map/ppermute | solution.py:44
  508.7 34.7 %collective-permute-start.63 = (bf16[512,512]{1,0:T(8,128)(2,1)S(1)}, bf16[512,512]{1,0:T(8,128)(2,1)S(1)}, u32[]{:S(2)}, u32[]{:S(2)}) collective-permute-start(bf16[512,512]{1,0:T(8,128)(2,1)S(1)} %get-tuple-element.105), channel_id=1, source_target_pairs={{3,0},{7,1},{0,2},{4,3},{1,4},{5,5},{2,6},{6,7},{11,8},{15,9},{8,1... | collective-permute-start | bytes 1572872 | tf_op jit(solution)/shard_map/ppermute | solution.py:44
  (80 other events, 1427.8 us)
Sparse Core Ops, SparseCore 0:
  161.1 33.7 all-gather.4
  262.7 47.6 all-gather.6
  393.1 59.0 all-gather.8
  512.5 32.2 all-gather.10
